TPU v7x, 512 devices: a whole 4x8x8 slice. The times are simulated.
512 devices in a mesh: row: 16 (over y, x_lo), col: 32 (over x_hi, z, core).
Axes of the slice: x: 4 (x_hi: 2, x_lo: 2; x = x_hi * 2 + x_lo), y: 8, z: 8, core: 2. Of those that a mesh axis runs over, the one named last changes fastest.
Arguments:
- tokens: bfloat16 [65536, 3584], P(('row', 'col')), may hold values from -6 to 6
- targets: bfloat16 [65536, 3584], P(('row', 'col')), may hold values from -6 to 6
- w_up: bfloat16 [32, 3584, 448], P('col', 'row'), may hold values from -6 to 6
- w_down: bfloat16 [16, 3584, 448], P('row', 'col'), may hold values from -6 to 6
- up_momentum: float32 [32, 3584, 448], P('col', 'row'), may hold values from -2 to 2
- down_momentum: float32 [16, 3584, 448], P('row', 'col'), may hold values from -2 to 2
- member_up: int32 [16, 32], replicated, may hold values from 0 to 1, as said below
- member_down: int32 [16, 32], replicated, may hold values from 0 to 1, as said below
- path_rate: float32 [16, 32], replicated, may hold values from 0.1 to 1
Outputs:
- new_up: bfloat16 [32, 3584, 448], P('col', 'row')
- new_up_momentum: float32 [32, 3584, 448], P('col', 'row')
- new_down: bfloat16 [16, 3584, 448], P('row', 'col')
- new_down_momentum: float32 [16, 3584, 448], P('row', 'col')
Inputs may be any that keep to these rules, and one draw needn't show every extreme that they name: Every column of member_up holds at least one 1. Every row of member_down holds at least one 1.
All inputs are finite; a program needn't handle non-finite values. Where the computation divides by a largest or mean magnitude, that divisor is 1e-20 or more.
Results may differ from a plain program's by a relative error of at most 0.006.
Values may be sent and summed in bfloat16 or wider, within the bound.
A program may use at most 64 MiB of HBM per device.

v0:
```python
import jax
import jax.numpy as jnp
from jax import lax
from jax.sharding import Mesh
from jax.sharding import PartitionSpec as P

ROW = ("row_0", "row_1")
ROW_COL = ("row_0", "row_1", "col")


def gathered_by_axis(x, axes, dim):
    filled = x
    for number in range(len(axes) - 1, -1, -1):
        filled = lax.all_gather(filled, axes[number], axis=dim, tiled=True)
    return filled


def joined_along(parts, dim):
    parts = jnp.moveaxis(parts, 0, dim)
    shape = parts.shape
    return parts.reshape(*shape[:dim], shape[dim] * shape[dim + 1], *shape[dim + 2 :])


def from_everyone(x, axis):
    peers = lax.axis_size(axis)
    return lax.all_to_all(jnp.broadcast_to(x[None], (peers, *x.shape)), axis, 0, 0, tiled=True)


def collect(x, axis, dim):
    return joined_along(from_everyone(x, axis), dim)


def silu_slope(pre):
    sig = jax.nn.sigmoid(pre)
    return sig * (1.0 + pre * (1.0 - sig))


def finish_forward(tokens, targets, pre, down_whole, inv_hidden):
    hidden_act = jax.nn.silu(pre).astype(jnp.bfloat16)
    mixed = (
        lax.dot_general(
            hidden_act, down_whole, (((1,), (1,)), ((), ())), preferred_element_type=jnp.float32
        )
        * inv_hidden
    )
    slope_out = (tokens.astype(jnp.float32) + mixed - targets.astype(jnp.float32)).astype(
        jnp.bfloat16
    )
    return (hidden_act, slope_out)


def packed(grad, rate):
    spread = jnp.sqrt(jnp.mean(grad * grad, axis=-1, keepdims=True) + 1e-05)
    unit = grad / (jnp.abs(grad) + spread)
    largest = jnp.max(jnp.abs(unit), axis=-1, keepdims=True) + 1e-06
    return ((unit / largest).astype(jnp.bfloat16), rate * largest[..., 0])


def owner_sum(weights, pieces):
    quant, scales = pieces
    factor = weights[:, None] * scales
    return jnp.sum(factor[:, :, None] * quant.astype(jnp.float32), axis=0)


def per_device(
    tokens, targets, w_up, w_down, up_momentum, down_momentum, member_up, member_down, path_rate
):
    width = tokens.shape[1]
    hidden = w_up.shape[2]
    rows = tokens.shape[0]
    inv_width = width ** (-0.5)
    inv_hidden = hidden ** (-0.5)
    row_index = lax.axis_index(ROW)
    col_index = lax.axis_index("col")
    row_count = lax.axis_size(ROW)
    col_count = lax.axis_size("col")
    rates_up = lax.dynamic_index_in_dim(path_rate, col_index, 1, False)
    rates_down = lax.dynamic_index_in_dim(path_rate, row_index, 0, False)
    down_whole = lax.all_gather(w_down[0], "col", axis=0, tiled=True)
    up_whole = gathered_by_axis(w_up[0], ROW, 0)
    pre = jnp.dot(tokens, up_whole, preferred_element_type=jnp.float32) * inv_width
    hidden_act, slope_out = finish_forward(tokens, targets, pre, down_whole, inv_hidden)
    slope_hidden = jnp.dot(slope_out, down_whole, preferred_element_type=jnp.float32) * inv_hidden
    slope_pre = (slope_hidden * silu_slope(pre)).astype(jnp.bfloat16)
    flags_up = lax.dynamic_index_in_dim(member_up, col_index, 1, False).astype(jnp.float32)
    weights_up = flags_up / jnp.sum(flags_up)
    input_parts = lax.all_to_all(
        tokens.reshape(rows, row_count, width // row_count),
        ROW,
        split_axis=1,
        concat_axis=1,
        tiled=True,
    )
    slope_parts = collect(slope_pre[None], ROW, 0)
    grads_owned = (
        jnp.einsum("rsk,srh->skh", input_parts, slope_parts, preferred_element_type=jnp.float32)
        * inv_width
    )
    quant_owned, scales_owned = packed(grads_owned, rates_up[:, None])
    average_up = owner_sum(weights_up, (quant_owned, scales_owned))
    momentum_first = 0.9 * up_momentum[0] + average_up
    fresh_up = (w_up[0].astype(jnp.float32) - 0.7 * (average_up + 0.9 * momentum_first)).astype(
        jnp.bfloat16
    )
    fresh_whole = gathered_by_axis(fresh_up, ROW, 0)
    pre_again = jnp.dot(tokens, fresh_whole, preferred_element_type=jnp.float32) * inv_width
    hidden_again, slope_again = finish_forward(tokens, targets, pre_again, down_whole, inv_hidden)
    flags_down = lax.dynamic_index_in_dim(member_down, row_index, 0, False).astype(jnp.float32)
    weights_down = flags_down / jnp.sum(flags_down)
    output_parts = lax.all_to_all(
        slope_again.reshape(rows, col_count, width // col_count),
        "col",
        split_axis=1,
        concat_axis=1,
        tiled=True,
    )
    hidden_parts = lax.all_gather(hidden_again[None], "col", axis=0, tiled=True)
    grads_down = (
        jnp.einsum("rsk,srh->skh", output_parts, hidden_parts, preferred_element_type=jnp.float32)
        * inv_hidden
    )
    quant_down, scales_down = packed(grads_down, rates_down[:, None])
    average_down = owner_sum(weights_down, (quant_down, scales_down))
    momentum_second = 0.9 * down_momentum[0] + average_down
    fresh_down = (
        w_down[0].astype(jnp.float32) - 0.7 * (average_down + 0.9 * momentum_second)
    ).astype(jnp.bfloat16)
    return (fresh_up[None], momentum_first[None], fresh_down[None], momentum_second[None])


def solution(mesh):
    torus = Mesh(mesh.devices.reshape(8, 2, mesh.shape["col"]), ("row_0", "row_1", "col"))
    placed = (
        P(ROW_COL, None),
        P(ROW_COL, None),
        P("col", ROW, None),
        P(ROW, "col", None),
        P("col", ROW, None),
        P(ROW, "col", None),
        P(),
        P(),
        P(),
    )
    return jax.shard_map(
        per_device,
        mesh=torus,
        in_specs=placed,
        out_specs=(
            P("col", ROW, None),
            P("col", ROW, None),
            P(ROW, "col", None),
            P(ROW, "col", None),
        ),
        check_vma=False,
    )
```

profile of v0, /device:TPU:1, one launch (start us, length us, event | category | flops | bytes accessed | tf_op | source)
XLA Modules:
  0.0 421.4 jit_solution(14377181742692491667)
XLA Ops:
  7.2 0.0 copy-start
  7.2 0.0 all-gather.11.cloned.1.call-start
  7.2 8.2 %all-gather = bf16[1,448,448]{2,1,0:T(8,128)(2,1)} all-gather(bf16[1,224,448]{2,1,0:T(8,128)(2,1)} %param.11), channel_id=2, replica_groups=mesh['row_0'=8,'row_1'=2,'col'=32] {'row_1'}, dimensions={1}, use_global_device_ids=true | all-gather | bytes 602112 | tf_op jit(solution)/shard_map/all_gather | solution.py:14
  15.4 0.0 all-gather.11.cloned.1.call-update
  15.5 0.0 all-gather.13.cloned.1.call-start
  15.5 0.7 all-gather.13.cloned.1.call-update
  16.2 2.2 copy.27
  18.4 8.8 %all-to-all-start.1 = ((bf16[128,16,224]{0,2,1:T(8,128)(2,1)}), bf16[128,16,224]{0,2,1:T(8,128)(2,1)S(1)}, u32[]{:S(2)}, u32[]{:S(2)}) async-start(bf16[128,16,224]{0,2,1:T(8,128)(2,1)} %bitcast.3), calls=%async_computation.1 | async-start | bytes 1835008 | tf_op jit(solution)/shard_map/all_to_all | solution.py:87
  27.3 58.7 %all-gather.11.cloned.1.call-done = bf16[1,3584,448]{2,1,0:T(8,128)(2,1)} async-done(((bf16[1,448,448]{2,1,0:T(8,128)(2,1)}), bf16[1,3584,448]{2,1,0:T(8,128)(2,1)}) %all-gather.11.cloned.1.call-update) | async-done | bytes 3211280 | tf_op jit(solution)/shard_map/all_gather | solution.py:14
  86.0 3.8 fusion.25
  89.8 93.1 %all-gather.13.cloned.1.call-done = bf16[1,3584,448]{2,1,0:T(8,128)(2,1)} async-done(((bf16[1,112,448]{2,1,0:T(8,128)(2,1)}), bf16[1,3584,448]{2,1,0:T(8,128)(2,1)}) %all-gather.13.cloned.1.call-update) | async-done | bytes 3211280 | tf_op jit(solution)/shard_map/all_gather | solution.py:79
  182.9 5.3 %fusion.39 = bf16[128,448]{0,1:T(8,128)(2,1)S(1)} fusion(bf16[1,3584,448]{2,1,0:T(8,128)(2,1)} %all-gather.13.cloned.1.call-done, bf16[128,3584]{1,0:T(8,128)(2,1)S(1)} %copy-done.2, bf16[128,3584]{1,0:T(8,128)(2,1)S(1)} %copy-done, f32[128,448]{0,1:T(8,128)S(1)} %fusion.25), kind=kOutput, calls=%fused_computation.40 | convolution fusion | flops 825696256 | bytes 5390336 | tf_op jit(solution)/shard_map/dot_general | solution.py:83
  188.3 1.6 broadcast_in_dim.4
  189.9 6.6 %all-to-all-start = ((bf16[16,1,128,448]{2,3,1,0:T(8,128)(2,1)}), bf16[16,1,128,448]{2,3,1,0:T(8,128)(2,1)S(1)}, u32[]{:S(2)}, u32[]{:S(2)}) async-start(bf16[16,1,128,448]{2,3,1,0:T(8,128)(2,1)} %broadcast_in_dim.4), calls=%async_computation | async-start | bytes 3670016 | tf_op jit(solution)/shard_map/all_to_all | solution.py:26
  196.4 0.0 all-gather.9.cloned.1.call-start
  196.5 1.1 copy.26
  197.6 1.2 copy.28
  198.8 0.7 convert_reduce_fusion
  199.5 0.8 dynamic-slice_reduce_fusion
  200.3 39.1 %all-to-all-done = bf16[16,1,128,448]{2,3,1,0:T(8,128)(2,1)S(1)} async-done(((bf16[16,1,128,448]{2,3,1,0:T(8,128)(2,1)}), bf16[16,1,128,448]{2,3,1,0:T(8,128)(2,1)S(1)}, u32[]{:S(2)}, u32[]{:S(2)}) %all-to-all-start) | async-done | bytes 1835040 | tf_op jit(solution)/shard_map/all_to_all | solution.py:26
  239.4 2.3 fusion.2
  241.7 2.0 fusion.5
  243.8 0.1 broadcast_add_fusion.1
  243.8 2.4 multiply_reduce_fusion.2
  246.2 0.1 fusion.47
  246.4 0.1 copy.29
  246.5 5.7 %all_gather.21 = bf16[448,448]{1,0:T(8,128)(2,1)} all-gather(bf16[224,448]{1,0:T(8,128)(2,1)S(1)} %copy.29), channel_id=1, replica_groups=mesh['row_0'=8,'row_1'=2,'col'=32] {'row_1'}, dimensions={0}, use_global_device_ids=true | all-gather | bytes 602112 | tf_op jit(solution)/shard_map/all_gather | solution.py:14
  252.1 0.0 all-gather.9.cloned.1.call-update
  252.2 0.2 all-gather.15.cloned.1.call-start
  252.4 50.7 %all-gather.9.cloned.1.call-done = bf16[3584,448]{1,0:T(8,128)(2,1)} async-done(((bf16[448,448]{1,0:T(8,128)(2,1)}), bf16[3584,448]{1,0:T(8,128)(2,1)}) %all-gather.9.cloned.1.call-update) | async-done | bytes 3211280 | tf_op jit(solution)/shard_map/all_gather | solution.py:14
  303.1 4.0 multiply_convert_fusion
  307.1 0.0 all-gather.15.cloned.1.call-update
  307.1 3.7 fusion.11
  310.9 1.3 copy.30
  312.2 10.6 %all-to-all-start.2 = ((bf16[128,32,112]{0,2,1:T(8,128)(2,1)}), bf16[128,32,112]{0,2,1:T(8,128)(2,1)S(1)}, u32[]{:S(2)}, u32[]{:S(2)}) async-start(bf16[128,32,112]{0,2,1:T(8,128)(2,1)} %bitcast.114), calls=%async_computation.2 | async-start | bytes 1835008 | tf_op jit(solution)/shard_map/all_to_all | solution.py:110
  322.8 1.3 fusion.68
  324.1 1.3 fusion.67
  325.4 0.1 bitcast_add_fusion.2
  325.6 0.8 copy.32
  326.4 1.0 copy.33
  327.3 25.0 %all-to-all-done.2 = bf16[128,32,112]{0,2,1:T(8,128)(2,1)S(1)} async-done(((bf16[128,32,112]{0,2,1:T(8,128)(2,1)}), bf16[128,32,112]{0,2,1:T(8,128)(2,1)S(1)}, u32[]{:S(2)}, u32[]{:S(2)}) %all-to-all-start.2) | async-done | bytes 917536 | tf_op jit(solution)/shard_map/all_to_all | solution.py:110
  352.4 51.8 %all-gather.15.cloned.1.call-done = bf16[4096,448]{0,1:T(8,128)(2,1)} async-done(((bf16[128,448]{0,1:T(8,128)(2,1)}), bf16[4096,448]{0,1:T(8,128)(2,1)}) %all-gather.15.cloned.1.call-update) | async-done | bytes 3670032 | tf_op jit(solution)/shard_map/all_gather | solution.py:117
  404.2 3.8 multiply_reduce_fusion.1
  408.0 0.0 copy-start.3
  408.0 3.1 abs_reduce_fusion
  411.1 0.1 broadcast_add_fusion
  411.2 2.8 multiply_reduce_fusion
  414.0 0.8 fusion.54
  (15 shorter events, 0.1 us)
Async XLA Ops:
  7.2 175.8 %copy-start = (bf16[128,3584]{1,0:T(8,128)(2,1)S(1)}, bf16[128,3584]{1,0:T(8,128)(2,1)}, u32[]{:S(2)}) copy-start(bf16[128,3584]{1,0:T(8,128)(2,1)} %param.9) | copy-start | bytes 2752516
  7.2 175.8 %copy-start.2 = (bf16[128,3584]{1,0:T(8,128)(2,1)S(1)}, bf16[128,3584]{1,0:T(8,128)(2,1)}, u32[]{:S(2)}) copy-start(bf16[128,3584]{1,0:T(8,128)(2,1)} %param.10) | copy-start | bytes 2752516
  7.2 78.8 %all-gather.11.cloned.1.call-start = ((), (), s32[]{:S(2)}) async-start(), calls=%async_computation.4 | async-start | bytes 4128768 | tf_op jit(solution)/shard_map/all_gather | solution.py:14
  15.5 167.5 %all-gather.13.cloned.1.call-start = ((), (), s32[]{:S(2)}) async-start(), calls=%async_computation.5 | async-start | bytes 3784704 | tf_op jit(solution)/shard_map/all_gather | solution.py:79
  18.4 169.8 %all-to-all-start.1 = ((bf16[128,16,224]{0,2,1:T(8,128)(2,1)}), bf16[128,16,224]{0,2,1:T(8,128)(2,1)S(1)}, u32[]{:S(2)}, u32[]{:S(2)}) async-start(bf16[128,16,224]{0,2,1:T(8,128)(2,1)} %bitcast.3), calls=%async_computation.1 | async-start | bytes 1835008 | tf_op jit(solution)/shard_map/all_to_all | solution.py:87
  89.8 109.0 %copy-start.5 = (s32[16,32]{1,0:T(8,128)S(1)}, s32[16,32]{1,0:T(8,128)}, u32[]{:S(2)}) copy-start(s32[16,32]{1,0:T(8,128)} %param.15) | copy-start | bytes 6148
  89.8 109.7 %copy-start.6 = (f32[16,32]{1,0:T(8,128)S(1)}, f32[16,32]{1,0:T(8,128)}, u32[]{:S(2)}) copy-start(f32[16,32]{1,0:T(8,128)} %param.17) | copy-start | bytes 6148
  188.3 1.6 copy-start.1
  189.9 49.5 %all-to-all-start = ((bf16[16,1,128,448]{2,3,1,0:T(8,128)(2,1)}), bf16[16,1,128,448]{2,3,1,0:T(8,128)(2,1)S(1)}, u32[]{:S(2)}, u32[]{:S(2)}) async-start(bf16[16,1,128,448]{2,3,1,0:T(8,128)(2,1)} %broadcast_in_dim.4), calls=%async_computation | async-start | bytes 3670016 | tf_op jit(solution)/shard_map/all_to_all | solution.py:26
  196.4 106.7 %all-gather.9.cloned.1.call-start = ((), (), s32[]{:S(2)}) async-start(), calls=%async_computation.3 | async-start | bytes 4128768 | tf_op jit(solution)/shard_map/all_gather | solution.py:14
  252.2 152.0 %all-gather.15.cloned.1.call-start = ((), (), s32[]{:S(2)}) async-start(), calls=%async_computation.6 | async-start | bytes 3784704 | tf_op jit(solution)/shard_map/all_gather | solution.py:117
  312.2 40.2 %all-to-all-start.2 = ((bf16[128,32,112]{0,2,1:T(8,128)(2,1)}), bf16[128,32,112]{0,2,1:T(8,128)(2,1)S(1)}, u32[]{:S(2)}, u32[]{:S(2)}) async-start(bf16[128,32,112]{0,2,1:T(8,128)(2,1)} %bitcast.114), calls=%async_computation.2 | async-start | bytes 1835008 | tf_op jit(solution)/shard_map/all_to_all | solution.py:110
  408.0 6.1 %copy-start.3 = (bf16[1,112,448]{2,1,0:T(8,128)(2,1)S(1)}, bf16[1,112,448]{2,1,0:T(8,128)(2,1)}, u32[]{:S(2)}) copy-start(bf16[1,112,448]{2,1,0:T(8,128)(2,1)} %param.12) | copy-start | bytes 301060
  408.0 6.1 %copy-start.4 = (f32[1,112,448]{2,1,0:T(8,128)S(1)}, f32[1,112,448]{2,1,0:T(8,128)}, u32[]{:S(2)}) copy-start(f32[1,112,448]{2,1,0:T(8,128)} %param.14) | copy-start | bytes 602116
Sparse Core Ops, SparseCore 0:
  15.6 70.3 all-gather.10
  89.3 93.5 all-gather.12
  252.3 50.7 all-gather.8
  307.3 96.8 all-gather.14
where the time goes:
time: 422 us; the launch traced here: 421 us
  waiting for transfers between devices  319 us (76%)
  starting transfers between devices  26.4 us (6%)
  matrix products  23 us (5%)
  other arithmetic  15.7 us (4%)
  between operations  14 us (3%)
  blocking collectives  13.9 us (3%)
  local copies, waits for them, and re-layouts  9.32 us (2%)
    all_gather x2, waiting for transfers between devices, gathered_by_axis(): filled = lax.all_gather(filled, axes[number], axis=dim, tiled=True)  109 us
    all_gather x1, waiting for transfers between devices, per_device(): down_whole = lax.all_gather(w_down[0], 'col', axis=0, tiled=True)  93.1 us
    all_gather x1, waiting for transfers between devices, per_device(): hidden_parts = lax.all_gather(hidden_again[None], 'col', axis=0, tiled=True)  51.8 us
    all_to_all x1, waiting for transfers between devices, from_everyone(): lax.all_to_all(jnp.broadcast_to(x[None], (peers, *x.shape)), axis, 0, 0,...  39.1 us
    all_to_all x1, waiting for transfers between devices, per_device(): lax.all_to_all(slope_again.reshape(rows, col_count, width // col_count),...  25 us
    all_gather x2, blocking collectives, gathered_by_axis(): filled = lax.all_gather(filled, axes[number], axis=dim, tiled=True)  13.9 us
    all_to_all x1, starting transfers between devices, per_device(): lax.all_to_all(slope_again.reshape(rows, col_count, width // col_count),...  10.6 us
    all_to_all x1, starting transfers between devices, per_device(): lax.all_to_all(tokens.reshape(rows, row_count, width // row_count), ROW,...  8.84 us
  transfers between devices with their start and end apart: 7, of which 6 were waited for; matrix products, arithmetic and copies ran while one was open for 6% of the time, Pallas kernels for 0%

commit v1 on v0

--- a/solution.py
+++ b/solution.py
@@ -65,6 +65,12 @@
 def per_device(
     tokens, targets, w_up, w_down, up_momentum, down_momentum, member_up, member_down, path_rate
 ):
+
+    def open_group(w_in, across):
+        return jnp.concatenate(
+            lax.all_to_all(jnp.stack([w_in] * lax.axis_size(across)), across, 0, 0), axis=0
+        )
+
     width = tokens.shape[1]
     hidden = w_up.shape[2]
     rows = tokens.shape[0]
@@ -76,7 +82,7 @@
     col_count = lax.axis_size("col")
     rates_up = lax.dynamic_index_in_dim(path_rate, col_index, 1, False)
     rates_down = lax.dynamic_index_in_dim(path_rate, row_index, 0, False)
-    down_whole = lax.all_gather(w_down[0], "col", axis=0, tiled=True)
+    down_whole = open_group(w_down[0], "col")
     up_whole = gathered_by_axis(w_up[0], ROW, 0)
     pre = jnp.dot(tokens, up_whole, preferred_element_type=jnp.float32) * inv_width
     hidden_act, slope_out = finish_forward(tokens, targets, pre, down_whole, inv_hidden)

time: 422 us -> 374 us (0.89)
  waiting for transfers between devices: 319 us -> 250 us
  starting transfers between devices: 26.4 us -> 38.4 us
  blocking collectives: 13.9 us -> 21.4 us
    all_gather x1 -> x0, waiting for transfers between devices: 93.1 us -> none  [per_device(): down_whole = lax.all_gather(w_down[0], 'col', axis=0, tiled=True)]
    all_to_all x0 -> x1, waiting for transfers between devices: none -> 67.8 us  [open_group(): lax.all_to_all(jnp.stack([w_in] * lax.axis_size(across)), across, 0, 0)]
    all_gather x2, waiting for transfers between devices: 109 us -> 53 us  [gathered_by_axis(): filled = lax.all_gather(filled, axes[number], axis=dim, tiled=True)]
    all_to_all x0 -> x1, starting transfers between devices: none -> 14.6 us  [open_group(): lax.all_to_all(jnp.stack([w_in] * lax.axis_size(across)), across, 0, 0)]
    all_to_all x1, waiting for transfers between devices: 0.01 us -> 14 us  [per_device(): lax.all_to_all(tokens.reshape(rows, row_count, width // row_count), ROW,...]
    all_gather x2, blocking collectives: 13.9 us -> 21.4 us  [gathered_by_axis(): filled = lax.all_gather(filled, axes[number], axis=dim, tiled=True)]
where the time goes in v1:
time: 374 us
  waiting for transfers between devices  250 us (67%)
  starting transfers between devices  38.4 us (10%)
  matrix products  22.7 us (6%)
  blocking collectives  21.4 us (6%)
  other arithmetic  15.6 us (4%)
  between operations  14 us (4%)
  local copies, waits for them, and re-layouts  11.6 us (3%)
    all_to_all x1, waiting for transfers between devices, open_group(): lax.all_to_all(jnp.stack([w_in] * lax.axis_size(across)), across, 0, 0)  67.8 us
    all_gather x2, waiting for transfers between devices, gathered_by_axis(): filled = lax.all_gather(filled, axes[number], axis=dim, tiled=True)  53 us
    all_gather x1, waiting for transfers between devices, per_device(): hidden_parts = lax.all_gather(hidden_again[None], 'col', axis=0, tiled=True)  51.8 us
    all_to_all x1, waiting for transfers between devices, from_everyone(): lax.all_to_all(jnp.broadcast_to(x[None], (peers, *x.shape)), axis, 0, 0,...  38 us
    all_to_all x1, waiting for transfers between devices, per_device(): lax.all_to_all(slope_again.reshape(rows, col_count, width // col_count),...  25 us
    all_gather x2, blocking collectives, gathered_by_axis(): filled = lax.all_gather(filled, axes[number], axis=dim, tiled=True)  21.4 us
    all_to_all x1, starting transfers between devices, open_group(): lax.all_to_all(jnp.stack([w_in] * lax.axis_size(across)), across, 0, 0)  14.6 us
    all_to_all x1, waiting for transfers between devices, per_device(): lax.all_to_all(tokens.reshape(rows, row_count, width // row_count), ROW,...  14 us
  transfers between devices with their start and end apart: 7, of which 6 were waited for; matrix products, arithmetic and copies ran while one was open for 6% of the time, Pallas kernels for 0%

profile of v1, /device:TPU:1, one launch (start us, length us, event | category | flops | bytes accessed | tf_op | source)
XLA Modules:
  0.0 373.6 jit_solution(14454274645998363263)
XLA Ops:
  7.2 0.0 copy-start.3
  7.2 3.2 stack.3
  10.4 14.6 %all-to-all-start = ((bf16[32,112,448]{2,1,0:T(8,128)(2,1)}), bf16[32,112,448]{2,1,0:T(8,128)(2,1)}, u32[]{:S(2)}, u32[]{:S(2)}) async-start(bf16[32,112,448]{2,1,0:T(8,128)(2,1)} %stack.3), calls=%async_computation | async-start | bytes 7340032 | tf_op jit(solution)/shard_map/all_to_all | solution.py:71
  25.0 0.0 all-gather.9.cloned.1.call-start
  25.1 15.8 %all-gather = bf16[1,448,448]{2,1,0:T(8,128)(2,1)} all-gather(bf16[1,224,448]{2,1,0:T(8,128)(2,1)S(1)} %copy-done.3), channel_id=2, replica_groups=mesh['row_0'=8,'row_1'=2,'col'=32] {'row_1'}, dimensions={1}, use_global_device_ids=true | all-gather | bytes 602112 | tf_op jit(solution)/shard_map/all_gather | solution.py:14
  40.9 0.0 all-gather.9.cloned.1.call-update
  40.9 1.3 copy.27
  42.2 67.8 %all-to-all-done = bf16[32,112,448]{2,1,0:T(8,128)(2,1)} async-done(((bf16[32,112,448]{2,1,0:T(8,128)(2,1)}), bf16[32,112,448]{2,1,0:T(8,128)(2,1)}, u32[]{:S(2)}, u32[]{:S(2)}) %all-to-all-start) | async-done | bytes 3211296 | tf_op jit(solution)/shard_map/all_to_all | solution.py:71
  110.0 7.0 %all-to-all-start.2 = ((bf16[128,16,224]{0,2,1:T(8,128)(2,1)}), bf16[128,16,224]{0,2,1:T(8,128)(2,1)S(1)}, u32[]{:S(2)}, u32[]{:S(2)}) async-start(bf16[128,16,224]{0,2,1:T(8,128)(2,1)} %bitcast.4), calls=%async_computation.2 | async-start | bytes 1835008 | tf_op jit(solution)/shard_map/all_to_all | solution.py:93
  117.0 0.0 all-gather.9.cloned.1.call-done
  117.0 3.5 fusion.19
  120.6 5.3 %fusion.24 = bf16[128,448]{0,1:T(8,128)(2,1)S(1)} fusion(bf16[3584,448]{1,0:T(8,128)(2,1)} %bitcast.2, bf16[128,3584]{1,0:T(8,128)(2,1)S(1)} %copy-done.2, bf16[128,3584]{1,0:T(8,128)(2,1)S(1)} %copy-done, f32[128,448]{0,1:T(8,128)S(1)} %fusion.19), kind=kOutput, calls=%fused_computation.36 | convolution fusion | flops 825696256 | bytes 5390336 | tf_op jit(solution)/shard_map/dot_general | solution.py:89
  125.9 14.0 %all-to-all-done.2 = bf16[128,16,224]{0,2,1:T(8,128)(2,1)S(1)} async-done(((bf16[128,16,224]{0,2,1:T(8,128)(2,1)}), bf16[128,16,224]{0,2,1:T(8,128)(2,1)S(1)}, u32[]{:S(2)}, u32[]{:S(2)}) %all-to-all-start.2) | async-done | bytes 917536 | tf_op jit(solution)/shard_map/all_to_all | solution.py:93
  139.9 1.6 broadcast_in_dim.4
  141.5 5.9 %all-to-all-start.1 = ((bf16[16,1,128,448]{2,3,1,0:T(8,128)(2,1)}), bf16[16,1,128,448]{2,3,1,0:T(8,128)(2,1)S(1)}, u32[]{:S(2)}, u32[]{:S(2)}) async-start(bf16[16,1,128,448]{2,3,1,0:T(8,128)(2,1)} %broadcast_in_dim.4), calls=%async_computation.1 | async-start | bytes 3670016 | tf_op jit(solution)/shard_map/all_to_all | solution.py:26
  147.4 0.0 all-gather.7.cloned.1.call-start
  147.5 1.1 copy.26
  148.6 1.2 copy.28
  149.8 0.7 convert_reduce_fusion
  150.5 0.8 dynamic-slice_reduce_fusion
  151.3 38.0 %all-to-all-done.1 = bf16[16,1,128,448]{2,3,1,0:T(8,128)(2,1)S(1)} async-done(((bf16[16,1,128,448]{2,3,1,0:T(8,128)(2,1)}), bf16[16,1,128,448]{2,3,1,0:T(8,128)(2,1)S(1)}, u32[]{:S(2)}, u32[]{:S(2)}) %all-to-all-start.1) | async-done | bytes 1835040 | tf_op jit(solution)/shard_map/all_to_all | solution.py:26
  189.3 2.3 fusion.2
  191.7 2.0 fusion.5
  193.7 0.1 broadcast_add_fusion.1
  193.8 2.4 multiply_reduce_fusion.2
  196.2 0.1 fusion.28
  196.3 0.1 copy.29
  196.4 5.7 %all_gather.17 = bf16[448,448]{1,0:T(8,128)(2,1)} all-gather(bf16[224,448]{1,0:T(8,128)(2,1)S(1)} %copy.29), channel_id=1, replica_groups=mesh['row_0'=8,'row_1'=2,'col'=32] {'row_1'}, dimensions={0}, use_global_device_ids=true | all-gather | bytes 602112 | tf_op jit(solution)/shard_map/all_gather | solution.py:14
  202.1 0.0 all-gather.7.cloned.1.call-update
  202.1 0.2 all-gather.11.cloned.1.call-start
  202.3 53.0 %all-gather.7.cloned.1.call-done = bf16[3584,448]{1,0:T(8,128)(2,1)} async-done(((bf16[448,448]{1,0:T(8,128)(2,1)}), bf16[3584,448]{1,0:T(8,128)(2,1)}) %all-gather.7.cloned.1.call-update) | async-done | bytes 3211280 | tf_op jit(solution)/shard_map/all_gather | solution.py:14
  255.3 4.0 %multiply_convert_fusion = bf16[128,448]{0,1:T(8,128)(2,1)} fusion(bf16[3584,448]{1,0:T(8,128)(2,1)} %all-gather.7.cloned.1.call-done, bf16[128,3584]{1,0:T(8,128)(2,1)S(1)} %copy-done), kind=kOutput, calls=%fused_computation.55 | convolution fusion | flops 411385856 | bytes 4243456 | tf_op jit(solution)/shard_map/dot_general | solution.py:112
  259.3 0.0 all-gather.11.cloned.1.call-update
  259.4 3.7 fusion.11
  263.1 1.3 copy.30
  264.4 10.6 %all-to-all-start.3 = ((bf16[128,32,112]{0,2,1:T(8,128)(2,1)}), bf16[128,32,112]{0,2,1:T(8,128)(2,1)S(1)}, u32[]{:S(2)}, u32[]{:S(2)}) async-start(bf16[128,32,112]{0,2,1:T(8,128)(2,1)} %bitcast.98), calls=%async_computation.3 | async-start | bytes 1835008 | tf_op jit(solution)/shard_map/all_to_all | solution.py:116
  275.0 1.3 fusion.49
  276.3 1.3 fusion.48
  277.7 0.1 bitcast_add_fusion.2
  277.8 0.8 copy.32
  278.6 1.0 copy.33
  279.6 25.0 %all-to-all-done.3 = bf16[128,32,112]{0,2,1:T(8,128)(2,1)S(1)} async-done(((bf16[128,32,112]{0,2,1:T(8,128)(2,1)}), bf16[128,32,112]{0,2,1:T(8,128)(2,1)S(1)}, u32[]{:S(2)}, u32[]{:S(2)}) %all-to-all-start.3) | async-done | bytes 917536 | tf_op jit(solution)/shard_map/all_to_all | solution.py:116
  304.6 51.8 %all-gather.11.cloned.1.call-done = bf16[4096,448]{0,1:T(8,128)(2,1)} async-done(((bf16[128,448]{0,1:T(8,128)(2,1)}), bf16[4096,448]{0,1:T(8,128)(2,1)}) %all-gather.11.cloned.1.call-update) | async-done | bytes 3670032 | tf_op jit(solution)/shard_map/all_gather | solution.py:123
  356.4 3.8 %multiply_reduce_fusion.1 = (f32[32,112]{1,0:T(8,128)S(1)}, f32[32,112,448]{2,1,0:T(8,128)S(1)}) fusion(bf16[128,32,112]{0,2,1:T(8,128)(2,1)S(1)} %all-to-all-done.3, bf16[4096,448]{0,1:T(8,128)(2,1)} %all-gather.11.cloned.1.call-done), kind=kOutput, calls=%fused_computation.11 | convolution fusion | flops 415855104 | bytes 11024384 | tf_op jit(solution)/shard_map/rsk,srh->skh/dot_general | solution.py:125
  360.2 3.1 abs_reduce_fusion
  363.4 0.1 broadcast_add_fusion
  363.4 2.8 multiply_reduce_fusion
  366.2 0.8 fusion.35
  (17 shorter events, 0.1 us)
Async XLA Ops:
  7.2 17.9 %copy-start.3 = (bf16[1,224,448]{2,1,0:T(8,128)(2,1)S(1)}, bf16[1,224,448]{2,1,0:T(8,128)(2,1)}, u32[]{:S(2)}) copy-start(bf16[1,224,448]{2,1,0:T(8,128)(2,1)} %param.11) | copy-start | bytes 602116
  7.2 33.7 %copy-start = (bf16[128,3584]{1,0:T(8,128)(2,1)S(1)}, bf16[128,3584]{1,0:T(8,128)(2,1)}, u32[]{:S(2)}) copy-start(bf16[128,3584]{1,0:T(8,128)(2,1)} %param.9) | copy-start | bytes 2752516
  10.4 110.1 %copy-start.2 = (bf16[128,3584]{1,0:T(8,128)(2,1)S(1)}, bf16[128,3584]{1,0:T(8,128)(2,1)}, u32[]{:S(2)}) copy-start(bf16[128,3584]{1,0:T(8,128)(2,1)} %param.10) | copy-start | bytes 2752516
  10.4 99.6 %all-to-all-start = ((bf16[32,112,448]{2,1,0:T(8,128)(2,1)}), bf16[32,112,448]{2,1,0:T(8,128)(2,1)}, u32[]{:S(2)}, u32[]{:S(2)}) async-start(bf16[32,112,448]{2,1,0:T(8,128)(2,1)} %stack.3), calls=%async_computation | async-start | bytes 7340032 | tf_op jit(solution)/shard_map/all_to_all | solution.py:71
  25.0 91.9 %all-gather.9.cloned.1.call-start = ((), (), s32[]{:S(2)}) async-start(), calls=%async_computation.5 | async-start | bytes 4128768 | tf_op jit(solution)/shard_map/all_gather | solution.py:14
  110.0 29.9 %all-to-all-start.2 = ((bf16[128,16,224]{0,2,1:T(8,128)(2,1)}), bf16[128,16,224]{0,2,1:T(8,128)(2,1)S(1)}, u32[]{:S(2)}, u32[]{:S(2)}) async-start(bf16[128,16,224]{0,2,1:T(8,128)(2,1)} %bitcast.4), calls=%async_computation.2 | async-start | bytes 1835008 | tf_op jit(solution)/shard_map/all_to_all | solution.py:93
  120.5 29.2 %copy-start.6 = (s32[16,32]{1,0:T(8,128)S(1)}, s32[16,32]{1,0:T(8,128)}, u32[]{:S(2)}) copy-start(s32[16,32]{1,0:T(8,128)} %param.15) | copy-start | bytes 6148
  120.5 29.9 %copy-start.7 = (f32[16,32]{1,0:T(8,128)S(1)}, f32[16,32]{1,0:T(8,128)}, u32[]{:S(2)}) copy-start(f32[16,32]{1,0:T(8,128)} %param.17) | copy-start | bytes 6148
  139.9 1.6 copy-start.1
  141.5 47.8 %all-to-all-start.1 = ((bf16[16,1,128,448]{2,3,1,0:T(8,128)(2,1)}), bf16[16,1,128,448]{2,3,1,0:T(8,128)(2,1)S(1)}, u32[]{:S(2)}, u32[]{:S(2)}) async-start(bf16[16,1,128,448]{2,3,1,0:T(8,128)(2,1)} %broadcast_in_dim.4), calls=%async_computation.1 | async-start | bytes 3670016 | tf_op jit(solution)/shard_map/all_to_all | solution.py:26
  147.4 107.9 %all-gather.7.cloned.1.call-start = ((), (), s32[]{:S(2)}) async-start(), calls=%async_computation.4 | async-start | bytes 4128768 | tf_op jit(solution)/shard_map/all_gather | solution.py:14
  202.1 154.3 %all-gather.11.cloned.1.call-start = ((), (), s32[]{:S(2)}) async-start(), calls=%async_computation.6 | async-start | bytes 3784704 | tf_op jit(solution)/shard_map/all_gather | solution.py:123
  264.4 40.2 %all-to-all-start.3 = ((bf16[128,32,112]{0,2,1:T(8,128)(2,1)}), bf16[128,32,112]{0,2,1:T(8,128)(2,1)S(1)}, u32[]{:S(2)}, u32[]{:S(2)}) async-start(bf16[128,32,112]{0,2,1:T(8,128)(2,1)} %bitcast.98), calls=%async_computation.3 | async-start | bytes 1835008 | tf_op jit(solution)/shard_map/all_to_all | solution.py:116
  360.2 6.0 %copy-start.4 = (bf16[1,112,448]{2,1,0:T(8,128)(2,1)S(1)}, bf16[1,112,448]{2,1,0:T(8,128)(2,1)}, u32[]{:S(2)}) copy-start(bf16[1,112,448]{2,1,0:T(8,128)(2,1)} %param.12) | copy-start | bytes 301060
  360.2 6.0 %copy-start.5 = (f32[1,112,448]{2,1,0:T(8,128)S(1)}, f32[1,112,448]{2,1,0:T(8,128)}, u32[]{:S(2)}) copy-start(f32[1,112,448]{2,1,0:T(8,128)} %param.14) | copy-start | bytes 602116
Sparse Core Ops, SparseCore 0:
  41.0 59.7 all-gather.8
  202.2 53.0 all-gather.6
  259.5 96.8 all-gather.10
